TPU v7x, 256 devices: a whole 4x4x8 slice. The times are simulated.
256 devices in a mesh: dp: 32 (over z, y_hi, core), tensor: 8 (over x, y_lo).
Axes of the slice: x: 4, y: 4 (y_hi: 2, y_lo: 2; y = y_hi * 2 + y_lo), z: 8, core: 2. Of those that a mesh axis runs over, the one named last changes fastest.
Arguments:
- activations: bfloat16 [16384, 18432], P('dp', 'tensor'), may hold values from -28 to 28
- old_codes: bfloat16 [2304, 8, 1024], P('dp', None, 'tensor'), may hold values from -1 to 1
- old_scales: float32 [2304, 8, 8], P('dp', None, 'tensor'), may hold values from 0.0002 to 0.002
Outputs:
- new_codes: bfloat16 [2304, 8, 1024], P('dp', None, 'tensor')
- new_scales: float32 [2304, 8, 8], P('dp', None, 'tensor')
All inputs are finite; a program needn't handle non-finite values. Where the computation divides by a largest or mean magnitude, that divisor is 1e-20 or more.
Results may differ from a plain program's by a relative error of at most 0.0015.
Values may be sent and summed in bfloat16 or wider, within the bound.
A program may use at most 64 MiB of HBM per device.

v0:
```python
import jax
import jax.numpy as jnp
from jax import lax
from jax.sharding import PartitionSpec as P

ROWB = 128
QB = 128


decay_rate = 0.95
contract = (((0,), (0,)), ((), ()))


def local(activations, old_codes, old_scales):
    tensor_count = lax.axis_size("tensor")
    tokens_all = activations.shape[0] * lax.axis_size("dp")
    block_width = activations.shape[1]
    window = activations[:, :ROWB]
    partial_value = lax.dot_general(
        lax.all_gather(activations, "tensor", axis=1, tiled=True),
        window,
        contract,
        preferred_element_type=jnp.float32,
    )
    partial_value = partial_value.reshape(tensor_count, block_width, ROWB)
    summed = lax.psum_scatter(partial_value, "dp", scatter_dimension=1, tiled=True)
    products = jnp.transpose(summed, (1, 0, 2))
    expand = jnp.repeat(old_scales, QB, axis=2)
    statistic = (
        decay_rate * old_codes.astype(jnp.float32) * expand
        + (1.0 - decay_rate) * products / tokens_all
    )
    blocks = statistic.reshape(statistic.shape[0], statistic.shape[1], ROWB // QB, QB)
    new_scales = jnp.max(jnp.abs(blocks), axis=3) + 1e-06
    new_codes = (blocks / new_scales[..., None]).reshape(statistic.shape).astype(jnp.bfloat16)
    return (new_codes, new_scales)


def solution(mesh):
    placed = (P("dp", "tensor"), P("dp", None, "tensor"), P("dp", None, "tensor"))
    return jax.shard_map(
        local,
        mesh=mesh,
        in_specs=placed,
        out_specs=(P("dp", None, "tensor"), P("dp", None, "tensor")),
        check_vma=False,
    )
```

profile of v0, /device:TPU:1, one launch (start us, length us, event | category | flops | bytes accessed | tf_op | source)
XLA Modules:
  0.0 570.5 jit_solution(5338898358822198367)
XLA Ops:
  7.2 0.0 all-gather.2.cloned.1.call-start
  7.2 0.7 all-gather.2.cloned.1.call-update
  7.9 0.0 reduce-scatter.2.cloned.1.call-start
  7.9 373.2 %all-gather.2.cloned.1.call-done = bf16[512,18432]{1,0:T(8,128)(2,1)} async-done(((bf16[512,2304]{1,0:T(8,128)(2,1)}), bf16[512,18432]{1,0:T(8,128)(2,1)}) %all-gather.2.cloned.1.call-update) | async-done | bytes 18874384 | tf_op jit(solution)/shard_map/all_gather | solution.py:20
  381.2 9.1 %fusion = f32[18432,128]{1,0:T(8,128)S(1)} fusion(bf16[512,18432]{1,0:T(8,128)(2,1)} %all-gather.2.cloned.1.call-done, bf16[512,2304]{1,0:T(8,128)(2,1)} %param.3), kind=kOutput, calls=%fused_computation.3 | convolution fusion | flops 2415919104 | bytes 28442624 | tf_op jit(solution)/shard_map/dot_general | solution.py:19
  390.3 13.9 %copy.9 = f32[8,2304,128]{2,0,1:T(8,128)} copy(f32[8,2304,128]{2,1,0:T(8,128)S(1)} %bitcast.11) | data formatting | bytes 18874368 | tf_op jit(solution)/shard_map/reshape | solution.py:25
  404.1 0.0 copy-start.1
  404.1 0.0 copy-start
  404.1 0.0 reduce-scatter.2.cloned.1.call-update
  404.2 0.7 copy-done.1
  404.8 0.1 copy.8
  404.9 155.0 %reduce-scatter.2.cloned.1.call-done = f32[8,72,128]{2,0,1:T(8,128)} async-done(((f32[8,2304,128]{2,0,1:T(8,128)}), f32[8,72,128]{2,0,1:T(8,128)}) %reduce-scatter.2.cloned.1.call-update) | async-done | bytes 294928 | tf_op jit(solution)/shard_map/reduce_scatter | solution.py:26
  559.9 0.0 copy-done
  559.9 1.2 abs_reduce_fusion
  561.1 0.7 copy.10
  561.8 1.8 divide_convert_fusion
  (2 shorter events, 0.0 us)
Async XLA Ops:
  7.2 374.0 %all-gather.2.cloned.1.call-start = ((), (), s32[]{:S(2)}) async-start(), calls=%async_computation.1 | async-start | bytes 21233664 | tf_op jit(solution)/shard_map/all_gather | solution.py:20
  7.9 552.0 %reduce-scatter.2.cloned.1.call-start = ((), (), s32[]{:S(2)}) async-start(), calls=%async_computation.2 | async-start | bytes 9732096 | tf_op jit(solution)/shard_map/reduce_scatter | solution.py:26
  404.1 0.7 copy-start.1
  404.1 155.8 %copy-start = (bf16[72,8,128]{2,1,0:T(8,128)(2,1)S(1)}, bf16[72,8,128]{2,1,0:T(8,128)(2,1)}, u32[]{:S(2)}) copy-start(bf16[72,8,128]{2,1,0:T(8,128)(2,1)} %param.4) | copy-start | bytes 442372
Sparse Core Ops, SparseCore 0:
  9.8 371.3 all-gather.1
  404.3 155.5 reduce-scatter.1
where the time goes:
time: 574 us; the launch traced here: 570 us
  waiting for transfers between devices  529 us (92%)
  local copies, waits for them, and re-layouts  15.3 us (3%)
  between operations  14.1 us (2%)
  matrix products  9.07 us (2%)
    all_gather x1, waiting for transfers between devices, local(): lax.all_gather(activations, 'tensor', axis=1, tiled=True)  373 us
    reduce_scatter x1, waiting for transfers between devices, local(): lax.psum_scatter(partial_value, 'dp', scatter_dimension=1, tiled=True)  155 us
    reshape x1, local copies, waits for them, and re-layouts, local(): partial_value = partial_value.reshape(tensor_count, block_width, ROWB)  13.9 us
  transfers between devices with their start and end apart: 2, of which 2 were waited for; matrix products, arithmetic and copies ran while one was open for 0% of the time, Pallas kernels for 0%

commit v1 on v0

--- a/solution.py
+++ b/solution.py
@@ -14,17 +14,14 @@
 def local(activations, old_codes, old_scales):
     tensor_count = lax.axis_size("tensor")
     tokens_all = activations.shape[0] * lax.axis_size("dp")
-    block_width = activations.shape[1]
-    window = activations[:, :ROWB]
+    windows = lax.all_gather(activations[:, :ROWB], "tensor", axis=1, tiled=True)
     partial_value = lax.dot_general(
-        lax.all_gather(activations, "tensor", axis=1, tiled=True),
-        window,
-        contract,
-        preferred_element_type=jnp.float32,
+        activations, windows, contract, preferred_element_type=jnp.float32
     )
-    partial_value = partial_value.reshape(tensor_count, block_width, ROWB)
-    summed = lax.psum_scatter(partial_value, "dp", scatter_dimension=1, tiled=True)
-    products = jnp.transpose(summed, (1, 0, 2))
+    summed = lax.psum_scatter(partial_value, "dp", scatter_dimension=0, tiled=True)
+    products = lax.all_to_all(
+        summed.reshape(summed.shape[0], tensor_count, ROWB), "tensor", 1, 1, tiled=False
+    )
     expand = jnp.repeat(old_scales, QB, axis=2)
     statistic = (
         decay_rate * old_codes.astype(jnp.float32) * expand

time: 574 us -> 249 us (0.43)
  waiting for transfers between devices: 529 us -> 213 us
  local copies, waits for them, and re-layouts: 15.3 us -> 4.75 us
    all_gather x1, waiting for transfers between devices: 373 us -> 45.2 us  [local(): lax.all_gather(activations[:, :ROWB], 'tensor', axis=1, tiled=True)]
    reshape x1, local copies, waits for them, and re-layouts: 13.9 us -> 1.69 us  [local(): summed.reshape(summed.shape[0], tensor_count, ROWB)]
    reduce_scatter x1, waiting for transfers between devices: 155 us -> 162 us  [local(): lax.psum_scatter(partial_value, 'dp', scatter_dimension=0, tiled=True)]
    all_to_all x0 -> x1, waiting for transfers between devices: none -> 5.9 us  [local(): lax.all_to_all(summed.reshape(summed.shape[0], tensor_count, ROWB), 'tens...]
  transfers between devices with their start and end apart: 2 -> 3, of which waited for: 2 -> 3; matrix products, arithmetic and copies ran while one was open for 0% -> 0% of each run, Pallas kernels for 0% -> 0%
where the time goes in v1:
time: 249 us; the launch traced here: 245 us
  waiting for transfers between devices  213 us (86%)
  between operations  14.1 us (6%)
  matrix products  8.2 us (3%)
  local copies, waits for them, and re-layouts  4.75 us (2%)
  starting transfers between devices  4.05 us (2%)
    reduce_scatter x1, waiting for transfers between devices, local(): lax.psum_scatter(partial_value, 'dp', scatter_dimension=0, tiled=True)  162 us
    all_gather x1, waiting for transfers between devices, local(): lax.all_gather(activations[:, :ROWB], 'tensor', axis=1, tiled=True)  45.2 us
    dot_general x1, matrix products, local(): lax.dot_general(activations, windows, contract, preferred_element_type=jn...  8.2 us
    all_to_all x1, waiting for transfers between devices, local(): lax.all_to_all(summed.reshape(summed.shape[0], tensor_count, ROWB), 'tens...  5.9 us
  transfers between devices with their start and end apart: 3, of which 3 were waited for; matrix products, arithmetic and copies ran while one was open for 0% of the time, Pallas kernels for 0%

profile of v1, /device:TPU:1, one launch (start us, length us, event | category | flops | bytes accessed | tf_op | source)
XLA Modules:
  0.0 244.6 jit_solution(17177402853799351065)
XLA Ops:
  7.2 0.0 all-gather.2.cloned.1.call-start
  7.2 1.6 slice.3
  8.8 0.0 all-gather.2.cloned.1.call-update
  8.8 0.0 reduce-scatter.2.cloned.1.call-start
  8.9 45.2 %all-gather.2.cloned.1.call-done = bf16[512,1024]{1,0:T(8,128)(2,1)} async-done(((bf16[512,128]{1,0:T(8,128)(2,1)}), bf16[512,1024]{1,0:T(8,128)(2,1)}) %all-gather.2.cloned.1.call-update) | async-done | bytes 1048592 | tf_op jit(solution)/shard_map/all_gather | solution.py:17
  54.0 8.2 %fusion.1 = f32[2304,1024]{1,0:T(8,128)} fusion(bf16[512,2304]{1,0:T(8,128)(2,1)} %param.3, bf16[512,1024]{1,0:T(8,128)(2,1)} %all-gather.2.cloned.1.call-done), kind=kOutput, calls=%fused_computation.7 | convolution fusion | flops 2415919104 | bytes 12845056 | tf_op jit(solution)/shard_map/dot_general | solution.py:18
  62.2 0.0 copy-start.1
  62.2 0.0 copy-start
  62.2 0.0 reduce-scatter.2.cloned.1.call-update
  62.3 161.8 %reduce-scatter.2.cloned.1.call-done = f32[72,1024]{1,0:T(8,128)} async-done(((f32[2304,1024]{1,0:T(8,128)}), f32[72,1024]{1,0:T(8,128)}) %reduce-scatter.2.cloned.1.call-update) | async-done | bytes 294928 | tf_op jit(solution)/shard_map/reduce_scatter | solution.py:21
  224.1 1.7 copy_bitcast_fusion
  225.8 4.0 %all-to-all-start = ((f32[72,8,128]{2,0,1:T(8,128)}), f32[72,8,128]{2,0,1:T(8,128)S(1)}, u32[]{:S(2)}, u32[]{:S(2)}) async-start(f32[72,8,128]{2,0,1:T(8,128)} %copy_bitcast_fusion), calls=%async_computation.1 | async-start | bytes 589824 | tf_op jit(solution)/shard_map/all_to_all | solution.py:22
  229.8 0.0 copy-done.1
  229.8 5.9 %all-to-all-done = f32[72,8,128]{2,0,1:T(8,128)S(1)} async-done(((f32[72,8,128]{2,0,1:T(8,128)}), f32[72,8,128]{2,0,1:T(8,128)S(1)}, u32[]{:S(2)}, u32[]{:S(2)}) %all-to-all-start) | async-done | bytes 294944 | tf_op jit(solution)/shard_map/all_to_all | solution.py:22
  235.7 0.0 copy-done
  235.7 0.3 abs_reduce_fusion
  236.0 0.1 copy.13
  236.1 0.1 copy.10
  236.2 0.2 divide_convert_fusion
  236.4 0.7 copy.11
  237.1 0.7 copy.12
  (2 shorter events, 0.0 us)
Async XLA Ops:
  7.2 46.9 %all-gather.2.cloned.1.call-start = ((), (), s32[]{:S(2)}) async-start(), calls=%async_computation.2 | async-start | bytes 1179648 | tf_op jit(solution)/shard_map/all_gather | solution.py:17
  8.8 215.3 %reduce-scatter.2.cloned.1.call-start = ((), (), s32[]{:S(2)}) async-start(), calls=%async_computation.3 | async-start | bytes 9732096 | tf_op jit(solution)/shard_map/reduce_scatter | solution.py:21
  62.2 167.5 %copy-start.1 = (f32[72,8,1]{0,2,1:T(1,128)S(1)}, f32[72,8,1]{0,2,1:T(1,128)}, u32[]{:S(2)}) copy-start(f32[72,8,1]{0,2,1:T(1,128)} %param.5) | copy-start | bytes 6916
  62.2 173.4 %copy-start = (bf16[72,8,128]{2,1,0:T(8,128)(2,1)S(1)}, bf16[72,8,128]{2,1,0:T(8,128)(2,1)}, u32[]{:S(2)}) copy-start(bf16[72,8,128]{2,1,0:T(8,128)(2,1)} %param.4) | copy-start | bytes 442372
  225.8 9.9 %all-to-all-start = ((f32[72,8,128]{2,0,1:T(8,128)}), f32[72,8,128]{2,0,1:T(8,128)S(1)}, u32[]{:S(2)}, u32[]{:S(2)}) async-start(f32[72,8,128]{2,0,1:T(8,128)} %copy_bitcast_fusion), calls=%async_computation.1 | async-start | bytes 589824 | tf_op jit(solution)/shard_map/all_to_all | solution.py:22
Sparse Core Ops, SparseCore 0:
  10.3 43.7 all-gather.1
  62.4 161.6 reduce-scatter.1

commit v2 on v1

v2 whole, which is shorter than its diff:
```python
import functools

import jax
import jax.numpy as jnp
from jax import lax
from jax.experimental import pallas as pl
from jax.experimental.pallas import tpu as pltpu
from jax.sharding import PartitionSpec as P

ROWB = 128
QB = 128
NX, NZ = 4, 8
SLAB = 144
HALF = 72
CODED = False

decay_rate = 0.95
MESH = pl.DeviceIdType.MESH

SHIFT = (0, 1, 3, 2)
CHAINS = (
    (0, False, True, 1),
    (0, False, False, 1),
    (1, True, False, -1),
    (2, True, False, 1),
    (3, False, True, -1),
    (3, False, False, -1),
)
TIMES = (
    (0.0, 4.0, 8.0, 12.0, 16.0),
    (0.1, 4.1, 8.1, 12.1, 16.1),
    (6.0, 9.5, 13.0, 16.5, 20.0),
    (15.0, 18.5, 22.0, 25.5, 29.0),
    (10.0, 14.0, 18.0, 22.0, 26.0),
    (10.1, 14.1, 18.1, 22.1, 26.1),
)
BUILD = (-1.0, 2.0, 5.0, 9.9)


def enc(v):
    return v


def dec(v):
    return v


def kernel(act, out, a_v, wown, at2, wbuf, p, zsend, zrecv, ysend, yrecv, rsend, rrecv, fbuf, frecv,
           hs_sem, a_ss, a_rs, w_ss, w_rs, v_ss, v_rs, z_ss, z_rs, y_ss, y_rs, r_ss, r_rs, f_ss, f_rs):
    d, t = lax.axis_index("dp"), lax.axis_index("tensor")
    x, l = t // 2, lax.rem(t, 2)
    z, h, c = d // 4, lax.rem(d // 2, 2), lax.rem(d, 2)

    def dev(dx=0, dz=0, hh=h, ll=l, cc=c):
        return {
            "dp": (lax.rem(z + dz + NZ, NZ) * 2 + hh) * 2 + cc,
            "tensor": lax.rem(x + dx, NX) * 2 + ll,
        }

    def remote(src, dst, ss, rs, to):
        return pltpu.make_async_remote_copy(
            src_ref=src, dst_ref=dst, send_sem=ss, recv_sem=rs, device_id=to, device_id_type=MESH
        )

    n_ch = a_ss.shape[0]
    width = a_v.shape[1]
    cw = width // n_ch
    load_w = pltpu.make_async_copy(act.at[:, pl.ds(0, ROWB)], wown, hs_sem.at[n_ch])
    load_w.start()
    loads = [
        pltpu.make_async_copy(
            act.at[:, pl.ds(i * cw, cw)], a_v.at[:, pl.ds(i * cw, cw)], hs_sem.at[i]
        )
        for i in range(n_ch)
    ]
    for cp in loads:
        cp.start()

    barrier = pltpu.get_barrier_semaphore()
    peers = [dev(dx, 0, h, lax.rem(l + dl, 2), lax.rem(c + dc, 2))
             for dx in range(NX) for dl in range(2) for dc in range(2) if dx or dl or dc]
    peers += [dev(dz=1), dev(dz=-1), dev(hh=1 - h)]
    for peer in peers:
        pl.semaphore_signal(barrier, inc=1, device_id=peer, device_id_type=MESH)
    pl.semaphore_wait(barrier, len(peers))

    sent = []
    load_w.wait()
    w_y = remote(wown, wbuf.at[0, c], w_ss.at[0], w_rs.at[c], dev(ll=1 - l, cc=l))
    w_y.start()
    sent.append(w_y)
    w_c = remote(wown, wbuf.at[0, c], w_ss.at[1], w_rs.at[c], dev(cc=1 - c))

    @pl.when(c != l)
    def _():
        w_c.start()

    @pl.when(c == l)
    def _():
        wbuf[0, c] = wown[...]

    swaps = []
    for i in range(n_ch):
        loads[i].wait()
        for b in range(cw // 128):
            lo = i * cw + b * 128
            at2[c, pl.ds(lo, 128), :] = a_v[:, lo:lo + 128].T
        part = at2.at[c, pl.ds(i * cw, cw), :]
        cp = remote(part, part, a_ss.at[i], a_rs.at[i], dev(cc=1 - c))
        cp.start()
        swaps.append(cp)
        if i == 0:
            w_in = remote(wown, wbuf.at[0, 1 - c], w_ss.at[0], w_rs.at[1 - c], dev(cc=1 - c))
            w_in.wait_recv()

            @pl.when(c != l)
            def _():
                w_y.wait_recv()

            win = {}
            for j, dx in ((1, 3), (2, 1), (3, 2)):
                win[j] = remote(wbuf.at[0], wbuf.at[j], v_ss.at[j], v_rs.at[j], dev(dx))
                win[j].start()
                sent.append(win[j])
    sent += swaps
    for cp in swaps:
        cp.wait_recv()

    def slab(off, other):
        hh = 1 - h if other else h
        return lax.rem(z + off + 2 * NZ, NZ) * 2 + hh

    def y_copy(q, n, src):
        return remote(src, yrecv.at[q, n], y_ss.at[q, n], y_rs.at[q, n], dev(hh=1 - h))

    def build(j, first, last):
        yfirst, sgn = [(ch[1], ch[3]) for ch in CHAINS if ch[0] == j][0]

        def body(n, carry):
            odd = lax.rem(n, 2)
            off = sgn * jnp.where(odd == 1, n // 2 - 3, 4 - n // 2)
            zs = lax.rem(z + off + 2 * NZ, NZ)
            rows = pl.ds(pl.multiple_of(zs * (2 * SLAB), 2 * SLAB), 2 * SLAB)
            res = jnp.dot(at2[0, rows, :], wbuf[j, 0], preferred_element_type=jnp.float32)
            res += jnp.dot(at2[1, rows, :], wbuf[j, 1], preferred_element_type=jnp.float32)
            p[j, zs * 2] = res[:SLAB]
            p[j, zs * 2 + 1] = res[SLAB:]
            if yfirst:
                q = j - 1
                if CODED:
                    ysend[q, n] = enc(p[j, zs * 2 + 1 - h])
                    y_copy(q, n, ysend.at[q, n]).start()
                else:
                    y_copy(q, n, p.at[j, zs * 2 + 1 - h]).start()
            return carry

        lax.fori_loop(first, last, body, 0)

    def z_copy(u, m, src, to):
        return remote(src, zrecv.at[u, m], z_ss.at[u, m], z_rs.at[u, m], dev(dz=to))

    def taken(u, m):
        j, yfirst, other, sgn = CHAINS[u]
        cp = z_copy(u, m, zsend.at[u, m] if CODED else p.at[j, slab(0, other)], sgn if m < 4 else -sgn)
        cp.wait_recv()
        return dec(zrecv[u, m])

    def own(u, n, off):
        j, yfirst, other, sgn = CHAINS[u]
        v = p[j, slab(off, other)]
        if yfirst:
            cp = y_copy(j - 1, n, ysend.at[j - 1, n] if CODED else p.at[j, slab(off, other)])
            cp.wait_recv()
            v = v + dec(yrecv[j - 1, n])
        return v

    def step(u, k):
        j, yfirst, other, sgn = CHAINS[u]
        todo = [(k, 2 * k, sgn * (4 - k), sgn)]
        if k < 3:
            todo.append((4 + k, 2 * k + 1, -sgn * (3 - k), -sgn))
        for m, n, off, to in todo:
            v = own(u, n, off)
            if k:
                v = v + taken(u, m - 1)
            if CODED:
                zsend[u, m] = enc(v)
                cp = z_copy(u, m, zsend.at[u, m], to)
            else:
                if k or yfirst:
                    p[j, slab(off, other)] = v
                cp = z_copy(u, m, p.at[j, slab(off, other)], to)
            cp.start()
            sent.append(cp)

    def spread(j, v):
        fbuf[j, 0] = v[:HALF]
        fbuf[j, 1] = v[HALF:]
        for cc in range(2):
            cp = remote(fbuf.at[j, cc], frecv.at[t], f_ss.at[j, cc], f_rs.at[t], dev(SHIFT[j], ll=c, cc=cc))
            if j:
                cp.start()
                sent.append(cp)
            else:
                away = jnp.logical_or(l != c, c != cc)

                @pl.when(away)
                def _():
                    cp.start()

                @pl.when(jnp.logical_not(away))
                def _():
                    frecv[t] = fbuf[0, cc]

                late.append((away, cp))

    late = []

    def finish(u):
        j, yfirst, other, sgn = CHAINS[u]
        v = own(u, 7, 0) + taken(u, 3) + taken(u, 6)
        if yfirst:
            spread(j, v)
            return
        q = j // 3
        cp = remote(rsend.at[q], rrecv.at[q], r_ss.at[q], r_rs.at[q], dev(hh=1 - h))
        if other:
            rsend[q] = v
            cp.start()
            sent.append(cp)
        else:
            cp.wait_recv()
            spread(j, v + rrecv[q])

    def arrive(j):
        if j:
            win[j].wait_recv()

    tasks = []
    for u, times in enumerate(TIMES):
        for k in range(4):
            tasks.append((times[k], functools.partial(step, u, k)))
        tasks.append((times[4], functools.partial(finish, u)))
    for j, when in enumerate(BUILD):
        tasks.append((when, functools.partial(arrive, j)))
        if j == 0 or j == 3:
            tasks.append((when + 0.001, functools.partial(build, j, 0, 2)))
            tasks.append((when + 1.5, functools.partial(build, j, 2, 8)))
        else:
            tasks.append((when + 0.001, functools.partial(build, j, 0, 8)))
    tasks.sort(key=lambda item: item[0])
    for _, run in tasks:
        run()

    for dx in range(NX):
        for ll in range(2):
            s = lax.rem(x + dx, NX) * 2 + lax.rem(l + ll, 2)
            cp = remote(fbuf.at[0, 0], frecv.at[s], f_ss.at[0, 0], f_rs.at[s], dev(cc=1 - c))
            if dx or ll:
                cp.wait_recv()
            else:
                pl.when(c != l)(cp.wait_recv)
    out[...] = frecv[...]

    for cp in sent:
        cp.wait_send()
    pl.when(c != l)(w_c.wait_send)
    for away, cp in late:
        pl.when(away)(cp.wait_send)
    for q in range(2):
        for n in range(8):
            y_copy(q, n, ysend.at[q, n] if CODED else p.at[q + 1, n]).wait_send()


def products_of(activations):
    tokens, width = activations.shape
    link = jnp.bfloat16 if CODED else jnp.float32
    dma = pltpu.SemaphoreType.DMA
    n_ch = 3
    small = (SLAB, ROWB)
    return pl.pallas_call(
        kernel,
        out_shape=jax.ShapeDtypeStruct((8, HALF, ROWB), jnp.float32),
        in_specs=[pl.BlockSpec(memory_space=pl.ANY)],
        out_specs=pl.BlockSpec(memory_space=pltpu.VMEM),
        scratch_shapes=[
            pltpu.VMEM((tokens, width), jnp.bfloat16),
            pltpu.VMEM((tokens, ROWB), jnp.bfloat16),
            pltpu.VMEM((2, width, tokens), jnp.bfloat16),
            pltpu.VMEM((4, 2, tokens, ROWB), jnp.bfloat16),
            pltpu.VMEM((4, 2 * NZ) + small, jnp.float32),
            pltpu.VMEM((6, 7) + small if CODED else (1, 1, 16, 128), link),
            pltpu.VMEM((6, 7) + small, link),
            pltpu.VMEM((2, 8) + small if CODED else (1, 1, 16, 128), link),
            pltpu.VMEM((2, 8) + small, link),
            pltpu.VMEM((2,) + small, jnp.float32),
            pltpu.VMEM((2,) + small, jnp.float32),
            pltpu.VMEM((4, 2, HALF, ROWB), jnp.float32),
            pltpu.VMEM((8, HALF, ROWB), jnp.float32),
            dma((n_ch + 1,)),
            dma((n_ch,)), dma((n_ch,)),
            dma((2,)), dma((2,)),
            dma((4,)), dma((4,)),
            dma((6, 7)), dma((6, 7)),
            dma((2, 8)), dma((2, 8)),
            dma((2,)), dma((2,)),
            dma((4, 2)), dma((8,)),
        ],
        compiler_params=pltpu.CompilerParams(
            collective_id=0, has_side_effects=True, vmem_limit_bytes=48 << 20
        ),
        name="summed_products",
    )(activations)


def local(activations, old_codes, old_scales):
    tokens_all = activations.shape[0] * lax.axis_size("dp")
    products = jnp.transpose(products_of(activations), (1, 0, 2))
    statistic = (
        decay_rate * old_codes.astype(jnp.float32) * old_scales
        + (1.0 - decay_rate) * products / tokens_all
    )
    new_scales = jnp.max(jnp.abs(statistic), axis=2, keepdims=True) + 1e-06
    new_codes = (statistic / new_scales).astype(jnp.bfloat16)
    return (new_codes, new_scales)


def solution(mesh):
    placed = (P("dp", "tensor"), P("dp", None, "tensor"), P("dp", None, "tensor"))
    return jax.shard_map(
        local,
        mesh=mesh,
        in_specs=placed,
        out_specs=(P("dp", None, "tensor"), P("dp", None, "tensor")),
        check_vma=False,
    )
```

time: 249 us -> 76.1 us (0.31); the launches traced: 245 us -> 75.7 us
  waiting for transfers between devices: 213 us -> 0 us
  Pallas kernels: 0 us -> 71.4 us
  between operations: 14.1 us -> 0.68 us
  matrix products: 8.2 us -> 0 us
  starting transfers between devices: 4.05 us -> 0 us
    reduce_scatter x1 -> x0, waiting for transfers between devices: 162 us -> none  [local(): lax.psum_scatter(partial_value, 'dp', scatter_dimension=0, tiled=True)]
    pallas_call x0 -> x1, Pallas kernels: none -> 71.4 us  [products_of(): pl.pallas_call(kernel, out_shape=jax.ShapeDtypeStruct((8, HALF, ROWB), jn...]
    all_gather x1 -> x0, waiting for transfers between devices: 45.2 us -> none  [local(): lax.all_gather(activations[:, :ROWB], 'tensor', axis=1, tiled=True)]
    dot_general x1 -> x0, matrix products: 8.2 us -> none  [local(): lax.dot_general(activations, windows, contract, preferred_element_type=jn...]
    all_to_all x1 -> x0, waiting for transfers between devices: 5.9 us -> none  [local(): lax.all_to_all(summed.reshape(summed.shape[0], tensor_count, ROWB), 'tens...]
    all_to_all x1 -> x0, starting transfers between devices: 3.97 us -> none  [local(): lax.all_to_all(summed.reshape(summed.shape[0], tensor_count, ROWB), 'tens...]
  transfers between devices with their start and end apart: 3 -> 0, of which waited for: 3 -> 0; matrix products, arithmetic and copies ran while one was open for 0% -> 0% of each run, Pallas kernels for 0% -> 0%
where the time goes in v2:
time: 76.1 us; the launch traced here: 75.7 us
  Pallas kernels  71.4 us (94%)
  local copies, waits for them, and re-layouts  2.36 us (3%)
  other arithmetic  1.24 us (2%)
    pallas_call x1, Pallas kernels, products_of(): pl.pallas_call(kernel, out_shape=jax.ShapeDtypeStruct((8, HALF, ROWB), jn...  71.4 us
    unnamed x7, local copies, waits for them, and re-layouts  2.36 us

profile of v2, /device:TPU:1, one launch (start us, length us, event | category | flops | bytes accessed | tf_op | source)
XLA Modules:
  0.0 75.7 jit_solution(15814848429930723903)
XLA Ops:
  0.6 0.7 broadcast_multiply_fusion
  1.3 0.0 copy-start
  1.3 1.7 %copy-done = bf16[512,2304]{1,0:T(8,128)(2,1)S(1)} copy-done((bf16[512,2304]{1,0:T(8,128)(2,1)S(1)}, bf16[512,2304]{1,0:T(8,128)(2,1)}, u32[]{:S(2)}) %copy-start) | copy-done | bytes 2359320
  3.0 0.0 copy-start.1
  3.0 71.4 %summed_products.1 = f32[8,72,128]{2,1,0:T(8,128)S(1)} custom-call(bf16[512,2304]{1,0:T(8,128)(2,1)S(1)} %copy-done), custom_call_target="tpu_custom_call" | custom-call | tf_op jit(solution)/shard_map/summed_products/pallas_call | solution.py:281
  74.4 0.0 copy-done.1
  74.4 0.3 abs_reduce_fusion
  74.7 0.0 copy-start.2
  74.7 0.2 divide_convert_fusion
  75.0 0.7 copy.6
  75.7 0.0 copy-done.2
  (1 shorter events, 0.0 us)
Async XLA Ops:
  1.3 1.7 %copy-start = (bf16[512,2304]{1,0:T(8,128)(2,1)S(1)}, bf16[512,2304]{1,0:T(8,128)(2,1)}, u32[]{:S(2)}) copy-start(bf16[512,2304]{1,0:T(8,128)(2,1)} %act.1) | copy-start | bytes 7077892
  3.0 71.4 %copy-start.1 = (bf16[72,8,128]{2,1,0:T(8,128)(2,1)S(1)}, bf16[72,8,128]{2,1,0:T(8,128)(2,1)}, u32[]{:S(2)}) copy-start(bf16[72,8,128]{2,1,0:T(8,128)(2,1)} %param.4) | copy-start | bytes 442372
  74.7 0.9 %copy-start.2 = (f32[72,8]{0,1:T(8,128)}, f32[72,8]{0,1:T(8,128)S(1)}, u32[]{:S(2)}) copy-start(f32[72,8]{0,1:T(8,128)S(1)} %broadcast_add_fusion) | copy-start | bytes 6916

commit v3 on v2

--- a/solution.py
+++ b/solution.py
@@ -1,4 +1,5 @@
 import functools
+import math
 
 import jax
 import jax.numpy as jnp
@@ -12,7 +13,7 @@
 NX, NZ = 4, 8
 SLAB = 144
 HALF = 72
-CODED = False
+CODED = True
 
 decay_rate = 0.95
 MESH = pl.DeviceIdType.MESH
@@ -37,12 +38,25 @@
 BUILD = (-1.0, 2.0, 5.0, 9.9)
 
 
+LEAST = 2.0 ** -5
+UNIT = 2.0 ** -9
+FLOOR = LEAST * (LEAST * UNIT) ** 7
+
+
 def enc(v):
-    return v
-
-
-def dec(v):
-    return v
+    if not CODED:
+        return v
+    a = jnp.maximum(jnp.abs(v), LEAST) * UNIT
+    a2 = a * a
+    return (v * ((a2 * a2) * (a2 * a))).astype(jnp.bfloat16)
+
+
+def dec(y):
+    if not CODED:
+        return y
+    y = y.astype(jnp.float32)
+    a = jnp.log(jnp.maximum(jnp.abs(y), FLOOR))
+    return y * jnp.exp(a * -0.875 + 0.875 * math.log(1.0 / UNIT))
 
 
 def kernel(act, out, a_v, wown, at2, wbuf, p, zsend, zrecv, ysend, yrecv, rsend, rrecv, fbuf, frecv,

time: 76.1 us -> 64.7 us (0.85)
  Pallas kernels: 71.4 us -> 60.3 us
    pallas_call x1, Pallas kernels: 71.4 us -> 60.3 us  [products_of(): pl.pallas_call(kernel, out_shape=jax.ShapeDtypeStruct((8, HALF, ROWB), jn...]
where the time goes in v3:
time: 64.7 us; the launch traced here: 64.5 us
  Pallas kernels  60.3 us (93%)
  local copies, waits for them, and re-layouts  2.36 us (4%)
  other arithmetic  1.24 us (2%)
  between operations  0.68 us (1%)
    pallas_call x1, Pallas kernels, products_of(): pl.pallas_call(kernel, out_shape=jax.ShapeDtypeStruct((8, HALF, ROWB), jn...  60.3 us
    unnamed x7, local copies, waits for them, and re-layouts  2.36 us

profile of v3, /device:TPU:1, one launch (start us, length us, event | category | flops | bytes accessed | tf_op | source)
XLA Modules:
  0.0 64.5 jit_solution(6331977996082425942)
XLA Ops:
  0.6 0.7 %broadcast_multiply_fusion = f32[72,8,1]{0,2,1:T(1,128)S(1)} fusion(f32[72,8,1]{0,2,1:T(1,128)} %param.5), kind=kLoop, calls=%fused_computation.4 | loop fusion | flops 576 | bytes 4608 | tf_op jit(solution)/shard_map/mul | solution.py:334
  1.3 0.0 copy-start
  1.3 1.7 %copy-done = bf16[512,2304]{1,0:T(8,128)(2,1)S(1)} copy-done((bf16[512,2304]{1,0:T(8,128)(2,1)S(1)}, bf16[512,2304]{1,0:T(8,128)(2,1)}, u32[]{:S(2)}) %copy-start) | copy-done | bytes 2359320
  3.0 0.0 copy-start.1
  3.0 60.3 %summed_products.1 = f32[8,72,128]{2,1,0:T(8,128)S(1)} custom-call(bf16[512,2304]{1,0:T(8,128)(2,1)S(1)} %copy-done), custom_call_target="tpu_custom_call" | custom-call | tf_op jit(solution)/shard_map/summed_products/pallas_call | solution.py:295
  63.3 0.0 copy-done.1
  63.3 0.3 abs_reduce_fusion
  63.6 0.0 copy-start.2
  63.6 0.2 divide_convert_fusion
  63.9 0.7 %copy.6 = bf16[72,8,128]{2,1,0:T(8,128)(2,1)} copy(bf16[72,8,128]{2,0,1:T(8,128)(2,1)S(1)} %divide_convert_fusion) | data formatting | bytes 294912
  64.5 0.0 copy-done.2
  (1 shorter events, 0.0 us)
Async XLA Ops:
  1.3 1.7 %copy-start = (bf16[512,2304]{1,0:T(8,128)(2,1)S(1)}, bf16[512,2304]{1,0:T(8,128)(2,1)}, u32[]{:S(2)}) copy-start(bf16[512,2304]{1,0:T(8,128)(2,1)} %act.1) | copy-start | bytes 7077892
  3.0 60.3 %copy-start.1 = (bf16[72,8,128]{2,1,0:T(8,128)(2,1)S(1)}, bf16[72,8,128]{2,1,0:T(8,128)(2,1)}, u32[]{:S(2)}) copy-start(bf16[72,8,128]{2,1,0:T(8,128)(2,1)} %param.4) | copy-start | bytes 442372
  63.6 0.9 %copy-start.2 = (f32[72,8]{0,1:T(8,128)}, f32[72,8]{0,1:T(8,128)S(1)}, u32[]{:S(2)}) copy-start(f32[72,8]{0,1:T(8,128)S(1)} %broadcast_add_fusion) | copy-start | bytes 6916

commit v4 on v1

v4 whole, which is shorter than its diff:
```python
import math

import jax
import jax.numpy as jnp
from jax import lax
from jax.experimental import pallas as pl
from jax.experimental.pallas import tpu as pltpu
from jax.sharding import PartitionSpec as P

ROWB = 128
QB = 128
NX, NZ = 4, 8
SLAB = 144
HALF = 72

decay_rate = 0.95
MESH = pl.DeviceIdType.MESH

OWNERS = (((0, 0), (1, 0), (2, 0), (3, 1)), ((3, 0), (0, 1), (1, 1), (2, 1)))
PLACE = {where: (core, j) for core in range(2) for j, where in enumerate(OWNERS[core])}
RING = ((4, 1), (-3, -1), (3, 1), (-2, -1), (2, 1), (-1, -1), (1, 1))
THREE = ((4, 1), (-3, -1), (2, 1), (3, 2), (-2, -1), (-1, -1), (1, 1))
TWO = ((4, 1), (2, 1), (-3, -1), (3, 3), (1, 1), (-2, -2), (-1, -1))
CHAINS = (
    (0, False, True, 1, THREE),
    (0, False, False, 1, THREE),
    (1, False, True, -1, RING),
    (1, False, False, -1, RING),
    (2, True, False, -1, THREE),
    (3, True, False, 1, TWO),
)
YFIRST = [j for j in range(4) if any(ch[0] == j and ch[1] for ch in CHAINS)]
HOPS = sorted({abs(hop) for ch in CHAINS for _, hop in ch[4]})
ORDER = (
    (0, 0, 0), (2, 0, 0), (3, 0, 0), (3, 1, 0), (3, 0, 1), (1, 0, 0), (2, 1, 0), (2, 0, 1), (3, 1, 1), (3, 2, 0),
    (3, 3, 0), (2, 1, 1), (3, 2, 1), (5, 0, 0), (2, 2, 0), (3, 3, 1), (2, 2, 1), (3, 0, 3), (3, 2, 2), (3, 0, 2),
    (3, 1, 3), (2, 3, 0), (3, 0, 4), (3, 1, 2), (2, 3, 1), (3, 3, 2), (3, 4, 0), (3, 4, 1), (3, 1, 4), (3, 2, 3),
    (3, 2, 4), (3, 3, 3), (3, 4, 2), (3, 3, 4), (3, 0, 5), (3, 4, 3), (3, 0, 6), (3, 1, 5), (3, 4, 4), (3, 1, 6),
    (3, 5, 0), (3, 2, 6), (3, 5, 1), (3, 2, 5), (3, 5, 2), (3, 3, 5), (3, 3, 6), (3, 4, 6), (4, 0, 0), (3, 5, 6),
    (3, 4, 5), (3, 5, 3), (3, 5, 4), (3, 5, 5), (4, 1, 0), (4, 2, 0), (4, 3, 0), (4, 4, 0), (4, 5, 0),
)

LEAST = 2.0 ** -5
UNIT = 2.0 ** -9
FLOOR = LEAST * (LEAST * UNIT) ** 7


def enc(v):
    a = jnp.maximum(jnp.abs(v), LEAST) * UNIT
    a2 = a * a
    return (v * ((a2 * a2) * (a2 * a))).astype(jnp.bfloat16)


def dec(y):
    y = y.astype(jnp.float32)
    a = jnp.log(jnp.maximum(jnp.abs(y), FLOOR))
    return y * jnp.exp(a * -0.875 + 0.875 * math.log(1.0 / UNIT))


def kernel(act, out, a_v, wown, wnext, at2, wbuf, p, zsend, zrecv, ysend, yrecv, fbuf, frecv,
           l_sem, a_ss, a_rs, w_ss, w_rs, n_ss, n_rs, z_ss, z_rs, y_ss, y_rs, f_ss, f_rs):
    d, t = lax.axis_index("dp"), lax.axis_index("tensor")
    x, l = t // 2, lax.rem(t, 2)
    z, h, c = d // 4, lax.rem(d // 2, 2), lax.rem(d, 2)

    def dev(dx=0, dz=0, hh=h, ll=l, cc=c):
        return {
            "dp": (lax.rem(z + dz + NZ, NZ) * 2 + hh) * 2 + cc,
            "tensor": lax.rem(x + dx + NX, NX) * 2 + ll,
        }

    def remote(src, dst, ss, rs, to):
        return pltpu.make_async_remote_copy(
            src_ref=src, dst_ref=dst, send_sem=ss, recv_sem=rs, device_id=to, device_id_type=MESH
        )

    def slab(off, other):
        return lax.rem(z + off + 2 * NZ, NZ) * 2 + (1 - h if other else h)

    def owner(j):
        (x0, l0), (x1, l1) = OWNERS[0][j], OWNERS[1][j]
        return x0 + c * (x1 - x0), lax.rem(l + l0 + c * (l1 - l0), 2)

    n_ch = l_sem.shape[0] - 1
    cw = a_v.shape[1] // n_ch
    load_w = pltpu.make_async_copy(act.at[:, pl.ds(0, ROWB)], wown, l_sem.at[n_ch])
    load_w.start()
    loads = []
    for i in range(n_ch):
        part = pl.ds(i * cw, cw)
        loads.append(pltpu.make_async_copy(act.at[:, part], a_v.at[:, part], l_sem.at[i]))
        loads[i].start()
    barrier = pltpu.get_barrier_semaphore()
    greet = [dev(dx, ll=lax.rem(l + dl, 2), cc=lax.rem(c + dc, 2))
             for dx in range(NX) for dl in range(2) for dc in range(2) if dx or dl or dc]
    greet += [dev(dz=s * hop) for hop in HOPS for s in (1, -1)]
    if YFIRST:
        greet.append(dev(hh=1 - h))
    for j, yfirst, other, _, _ in CHAINS:
        if other:
            greet += [dev(-dx, hh=1 - h, ll=lax.rem(l + dl, 2), cc=core)
                      for core in range(2) for dx, dl in (OWNERS[core][j],)]
    for peer in greet:
        pl.semaphore_signal(barrier, inc=1, device_id=peer, device_id_type=MESH)
    for i in range(n_ch):
        loads[i].wait()
        for b in range(cw // 128):
            lo = i * cw + b * 128
            at2[c, pl.ds(lo, 128), :] = a_v[:, lo:lo + 128].T
    load_w.wait()
    pl.semaphore_wait(barrier, len(greet))

    sent = []

    def go(cp):
        cp.start()
        sent.append(cp)

    def share(src, dl, dx):
        core, j = PLACE[dx, dl]
        return remote(src, wbuf.at[j, c], w_ss.at[dl, dx], w_rs.at[j, c], dev(-dx, cc=core))

    def share_here(src, dl):
        core, j = PLACE[0, dl]
        cp = share(src, dl, 0)
        pl.when(c != core)(cp.start)

        @pl.when(c == core)
        def _():
            wbuf[j, core] = src[...]

        late.append((c != core, cp))

    late = []
    w_y = remote(wown, wnext, n_ss, n_rs, dev(ll=1 - l))
    go(w_y)
    go(share(wown, 0, 1))
    go(share(wown, 0, 3))
    share_here(wown, 0)

    swaps = []
    for n in range(NZ):
        zs = lax.rem(z + (n // 2 - 3 if n % 2 else 4 - n // 2) + NZ, NZ)
        part = at2.at[c, pl.ds(pl.multiple_of(zs * (2 * SLAB), 2 * SLAB), 2 * SLAB), :]
        swaps.append(remote(part, part, a_ss.at[n], a_rs.at[n], dev(cc=1 - c)))
        go(swaps[n])
    here = set()

    def need_swaps(upto):
        for n in range(upto):
            if n not in here:
                here.add(n)
                swaps[n].wait_recv()

    def windows(kind):
        if kind == 0:
            go(share(wown, 0, 2))
        elif kind == 1:
            w_y.wait_recv()
            go(share(wnext, 1, 1))
            go(share(wnext, 1, 3))
            share_here(wnext, 1)
        else:
            go(share(wnext, 1, 2))

    def windows_in(j):
        for half in range(2):
            cp = remote(wown, wbuf.at[j, half], w_ss.at[0, 0], w_rs.at[j, half], dev(cc=1 - c))
            own = [core for core in range(2) if OWNERS[core][j][0] == 0 and core == half]
            if own:
                pl.when(c != own[0])(cp.wait_recv)
            else:
                cp.wait_recv()

    def plan_of(j):
        return [ch for ch in CHAINS if ch[0] == j][0]

    def y_copy(q, n):
        return remote(ysend.at[q, n], yrecv.at[q, n], y_ss.at[q, n], y_rs.at[q, n], dev(hh=1 - h))

    def build(j, part):
        _, yfirst, _, sgn, plan = plan_of(j)
        first, last = ((0, 2), (2, 8))[part]
        if part == 0:
            windows_in(j)
        offs = [off * sgn for off, _ in plan] + [0]
        near = {0: 2, 1: 8}[part] if sgn == 1 and plan[:2] == RING[:2] else 8
        need_swaps(near)
        for n in range(first, last):
            zs = lax.rem(z + offs[n] + NZ, NZ)
            rows = pl.ds(pl.multiple_of(zs * (2 * SLAB), 2 * SLAB), 2 * SLAB)
            res = jnp.dot(at2[0, rows, :], wbuf[j, 0], preferred_element_type=jnp.float32)
            res += jnp.dot(at2[1, rows, :], wbuf[j, 1], preferred_element_type=jnp.float32)
            p[j, zs * 2] = res[:SLAB]
            p[j, zs * 2 + 1] = res[SLAB:]
            if yfirst:
                q = YFIRST.index(j)
                ysend[q, n] = enc(p[j, zs * 2 + 1 - h])
                y_copy(q, n).start()

    def z_copy(u, i, hop):
        return remote(zsend.at[u, i], zrecv.at[u, i], z_ss.at[u, i], z_rs.at[u, i], dev(dz=hop))

    def gathered(u, n, off):
        j, yfirst, other, sgn, plan = CHAINS[u]
        v = p[j, slab(off * sgn, other)]
        if yfirst:
            y_copy(YFIRST.index(j), n).wait_recv()
            v = v + dec(yrecv[YFIRST.index(j), n])
        for k, (o, hop) in enumerate(plan):
            if o - hop == off:
                z_copy(u, k, hop * sgn).wait_recv()
                v = v + dec(zrecv[u, k])
        return v

    def pass_on(u, i):
        sgn, plan = CHAINS[u][3:]
        off, hop = plan[i]
        zsend[u, i] = enc(gathered(u, i, off))
        go(z_copy(u, i, hop * sgn))

    def f_copy(u, cc, slot):
        j, _, other, _, _ = CHAINS[u]
        dx, ll = owner(j)
        to = dev(dx, hh=1 - h if other else h, ll=ll, cc=cc)
        return remote(fbuf.at[u, cc], frecv.at[slot, t], f_ss.at[u, cc], f_rs.at[slot, t], to)

    def finish(u, _):
        j, yfirst, other, sgn, plan = CHAINS[u]
        v = gathered(u, 7, 0)
        fbuf[u, 0] = v[:HALF]
        fbuf[u, 1] = v[HALF:]
        for cc in range(2):
            cp = f_copy(u, cc, int(other))
            here_on = [core for core in range(2) if OWNERS[core][j] == (0, 0) and core == cc and not other]
            if not here_on:
                go(cp)
                continue
            pl.when(c != here_on[0])(cp.start)

            @pl.when(c == here_on[0])
            def _():
                frecv[0, t] = fbuf[u, cc]

            late.append((c != here_on[0], cp))

    for kind, one, two in ORDER:
        if kind in (0, 1, 5):
            windows(kind)
        else:
            (build, pass_on, finish)[kind - 2](one, two)

    for (dx, dl), (core, j) in PLACE.items():
        twice = any(ch[0] == j and ch[2] for ch in CHAINS)
        s = lax.rem(x - dx + NX, NX) * 2 + lax.rem(l + dl, 2)
        for slot in range(1 + twice):
            cp = remote(fbuf.at[0, 0], frecv.at[slot, s], f_ss.at[0, 0], f_rs.at[slot, s], dev(cc=1 - c))
            if dx or dl or slot:
                cp.wait_recv()
            else:
                pl.when(c != core)(cp.wait_recv)
        out[s] = frecv[0, s] + frecv[1, s] if twice else frecv[0, s]

    for cp in sent:
        cp.wait_send()
    for away, cp in late:
        pl.when(away)(cp.wait_send)
    for q in range(len(YFIRST)):
        for n in range(8):
            y_copy(q, n).wait_send()


def products_of(activations):
    tokens, width = activations.shape
    dma = pltpu.SemaphoreType.DMA
    n_ch = 3
    small = (SLAB, ROWB)
    n_u, n_y = len(CHAINS), max(len(YFIRST), 1)
    return pl.pallas_call(
        kernel,
        out_shape=jax.ShapeDtypeStruct((8, HALF, ROWB), jnp.float32),
        in_specs=[pl.BlockSpec(memory_space=pltpu.HBM)],
        out_specs=pl.BlockSpec(memory_space=pltpu.VMEM),
        scratch_shapes=[
            pltpu.VMEM((tokens, width), jnp.bfloat16),
            pltpu.VMEM((tokens, ROWB), jnp.bfloat16),
            pltpu.VMEM((tokens, ROWB), jnp.bfloat16),
            pltpu.VMEM((2, width, tokens), jnp.bfloat16),
            pltpu.VMEM((4, 2, tokens, ROWB), jnp.bfloat16),
            pltpu.VMEM((4, 2 * NZ) + small, jnp.float32),
            pltpu.VMEM((n_u, 7) + small, jnp.bfloat16),
            pltpu.VMEM((n_u, 7) + small, jnp.bfloat16),
            pltpu.VMEM((n_y, 8) + small, jnp.bfloat16),
            pltpu.VMEM((n_y, 8) + small, jnp.bfloat16),
            pltpu.VMEM((n_u, 2, HALF, ROWB), jnp.float32),
            pltpu.VMEM((2, 8, HALF, ROWB), jnp.float32),
            dma((n_ch + 1,)),
            dma((NZ,)), dma((NZ,)),
            dma((2, 4)), dma((4, 2)),
            dma, dma,
            dma((n_u, 7)), dma((n_u, 7)),
            dma((n_y, 8)), dma((n_y, 8)),
            dma((n_u, 2)), dma((2, 8)),
        ],
        compiler_params=pltpu.CompilerParams(
            collective_id=0, has_side_effects=True, vmem_limit_bytes=52 << 20
        ),
        name="summed_products",
    )(activations)


def local(activations, old_codes, old_scales):
    tokens_all = activations.shape[0] * lax.axis_size("dp")
    products = jnp.transpose(products_of(activations), (1, 0, 2))
    products, old_codes, old_scales = lax.optimization_barrier((products, old_codes, old_scales))
    statistic = (
        decay_rate * old_codes.astype(jnp.float32) * old_scales
        + (1.0 - decay_rate) * products / tokens_all
    )
    new_scales = jnp.max(jnp.abs(statistic), axis=2, keepdims=True) + 1e-06
    new_codes = (statistic / new_scales).astype(jnp.bfloat16)
    return (new_codes, new_scales)


def solution(mesh):
    placed = (P("dp", "tensor"), P("dp", None, "tensor"), P("dp", None, "tensor"))
    return jax.shard_map(
        local,
        mesh=mesh,
        in_specs=placed,
        out_specs=(P("dp", None, "tensor"), P("dp", None, "tensor")),
        check_vma=False,
    )
```

time: 249 us -> 52.2 us (0.21)
  the two profiles are of different devices: /device:TPU:1 before, /device:TPU:3 now
where the time goes in v4:
time: 52.2 us; the launch traced here: 52.1 us
  Pallas kernels  50.1 us (96%)
  between operations  0.71 us (1%)
  local copies, waits for them, and re-layouts  0.7 us (1%)
  other arithmetic  0.56 us (1%)
    pallas_call x1, Pallas kernels, products_of(): pl.pallas_call(kernel, out_shape=jax.ShapeDtypeStruct((8, HALF, ROWB), jn...  50.1 us

profile of v4, /device:TPU:3, one launch (start us, length us, event | category | flops | bytes accessed | tf_op | source)
XLA Modules:
  0.0 52.1 jit_solution(9294593688374877502)
XLA Ops:
  0.6 0.0 copy-start.2
  0.6 0.0 copy-start
  0.6 50.1 %summed_products.1 = f32[8,72,128]{2,1,0:T(8,128)S(1)} custom-call(bf16[512,2304]{1,0:T(8,128)(2,1)} %act.1), custom_call_target="tpu_custom_call" | custom-call | tf_op jit(solution)/shard_map/summed_products/pallas_call | solution.py:279
  50.8 0.0 copy-done.2
  50.8 0.0 copy-done
  50.8 0.3 abs_reduce_fusion
  51.2 0.0 copy-start.1
  51.2 0.2 divide_convert_fusion
  51.4 0.7 %copy.6 = bf16[72,8,128]{2,1,0:T(8,128)(2,1)} copy(bf16[72,8,128]{2,0,1:T(8,128)(2,1)S(1)} %divide_convert_fusion) | data formatting | bytes 294912
  52.1 0.0 copy-done.1
  (2 shorter events, 0.0 us)
Async XLA Ops:
  0.6 50.2 %copy-start.2 = (f32[72,8,1]{0,2,1:T(1,128)S(1)}, f32[72,8,1]{0,2,1:T(1,128)}, u32[]{:S(2)}) copy-start(f32[72,8,1]{0,2,1:T(1,128)} %param.5) | copy-start | bytes 6916
  0.6 50.2 %copy-start = (bf16[72,8,128]{2,1,0:T(8,128)(2,1)S(1)}, bf16[72,8,128]{2,1,0:T(8,128)(2,1)}, u32[]{:S(2)}) copy-start(bf16[72,8,128]{2,1,0:T(8,128)(2,1)} %param.4) | copy-start | bytes 442372
  51.2 0.9 %copy-start.1 = (f32[72,8]{0,1:T(8,128)}, f32[72,8]{0,1:T(8,128)S(1)}, u32[]{:S(2)}) copy-start(f32[72,8]{0,1:T(8,128)S(1)} %broadcast_add_fusion) | copy-start | bytes 6916

commit v5 on v4

--- a/solution.py
+++ b/solution.py
@@ -12,6 +12,7 @@
 NX, NZ = 4, 8
 SLAB = 144
 HALF = 72
+STRIP = 144
 
 decay_rate = 0.95
 MESH = pl.DeviceIdType.MESH
@@ -32,12 +33,12 @@
 YFIRST = [j for j in range(4) if any(ch[0] == j and ch[1] for ch in CHAINS)]
 HOPS = sorted({abs(hop) for ch in CHAINS for _, hop in ch[4]})
 ORDER = (
-    (0, 0, 0), (2, 0, 0), (3, 0, 0), (3, 1, 0), (3, 0, 1), (1, 0, 0), (2, 1, 0), (2, 0, 1), (3, 1, 1), (3, 2, 0),
-    (3, 3, 0), (2, 1, 1), (3, 2, 1), (5, 0, 0), (2, 2, 0), (3, 3, 1), (2, 2, 1), (3, 0, 3), (3, 2, 2), (3, 0, 2),
-    (3, 1, 3), (2, 3, 0), (3, 0, 4), (3, 1, 2), (2, 3, 1), (3, 3, 2), (3, 4, 0), (3, 4, 1), (3, 1, 4), (3, 2, 3),
-    (3, 2, 4), (3, 3, 3), (3, 4, 2), (3, 3, 4), (3, 0, 5), (3, 4, 3), (3, 0, 6), (3, 1, 5), (3, 4, 4), (3, 1, 6),
-    (3, 5, 0), (3, 2, 6), (3, 5, 1), (3, 2, 5), (3, 5, 2), (3, 3, 5), (3, 3, 6), (3, 4, 6), (4, 0, 0), (3, 5, 6),
-    (3, 4, 5), (3, 5, 3), (3, 5, 4), (3, 5, 5), (4, 1, 0), (4, 2, 0), (4, 3, 0), (4, 4, 0), (4, 5, 0),
+    (0, 0, 0), (1, 0, 0), (2, 0, 0), (3, 0, 0), (3, 0, 1), (3, 1, 0), (2, 1, 0), (3, 1, 1), (3, 3, 1), (3, 2, 0),
+    (2, 0, 1), (3, 3, 0), (3, 1, 2), (3, 0, 2), (2, 1, 1), (3, 0, 3), (3, 0, 4), (3, 1, 3), (5, 0, 0), (3, 2, 1),
+    (3, 1, 4), (2, 2, 0), (3, 3, 2), (2, 2, 1), (3, 2, 2), (3, 3, 3), (2, 3, 0), (3, 0, 5), (3, 1, 5), (3, 2, 3),
+    (3, 0, 6), (3, 4, 0), (3, 3, 4), (3, 4, 1), (2, 3, 1), (3, 2, 4), (3, 4, 2), (3, 1, 6), (3, 2, 5), (3, 4, 3),
+    (3, 5, 0), (3, 4, 4), (3, 5, 2), (3, 5, 1), (4, 0, 0), (3, 2, 6), (3, 3, 6), (3, 3, 5), (3, 5, 3), (3, 5, 6),
+    (4, 1, 0), (3, 4, 6), (3, 4, 5), (3, 5, 5), (3, 5, 4), (4, 3, 0), (4, 2, 0), (4, 4, 0), (4, 5, 0),
 )
 
 LEAST = 2.0 ** -5
@@ -104,9 +105,12 @@
         pl.semaphore_signal(barrier, inc=1, device_id=peer, device_id_type=MESH)
     for i in range(n_ch):
         loads[i].wait()
-        for b in range(cw // 128):
-            lo = i * cw + b * 128
-            at2[c, pl.ds(lo, 128), :] = a_v[:, lo:lo + 128].T
+
+        @pl.loop(0, cw // 128)
+        def _(b):
+            part = pl.ds(pl.multiple_of(i * cw + b * 128, 128), 128)
+            at2[c, part, :] = a_v[:, part].T
+
     load_w.wait()
     pl.semaphore_wait(barrier, len(greet))
 
@@ -134,8 +138,9 @@
     late = []
     w_y = remote(wown, wnext, n_ss, n_rs, dev(ll=1 - l))
     go(w_y)
-    go(share(wown, 0, 1))
-    go(share(wown, 0, 3))
+    near = [share(wown, 0, 1), share(wown, 0, 3)]
+    for cp in near:
+        cp.start()
     share_here(wown, 0)
 
     swaps = []
@@ -154,6 +159,8 @@
 
     def windows(kind):
         if kind == 0:
+            for cp in near:
+                cp.wait_send()
             go(share(wown, 0, 2))
         elif kind == 1:
             w_y.wait_recv()
@@ -186,8 +193,13 @@
         offs = [off * sgn for off, _ in plan] + [0]
         near = {0: 2, 1: 8}[part] if sgn == 1 and plan[:2] == RING[:2] else 8
         need_swaps(near)
-        for n in range(first, last):
-            zs = lax.rem(z + offs[n] + NZ, NZ)
+
+        @pl.loop(first, last)
+        def _(n):
+            off = offs[-1]
+            for i in range(7):
+                off = jnp.where(n == i, offs[i], off)
+            zs = lax.rem(z + off + NZ, NZ)
             rows = pl.ds(pl.multiple_of(zs * (2 * SLAB), 2 * SLAB), 2 * SLAB)
             res = jnp.dot(at2[0, rows, :], wbuf[j, 0], preferred_element_type=jnp.float32)
             res += jnp.dot(at2[1, rows, :], wbuf[j, 1], preferred_element_type=jnp.float32)
@@ -195,41 +207,60 @@
             p[j, zs * 2 + 1] = res[SLAB:]
             if yfirst:
                 q = YFIRST.index(j)
-                ysend[q, n] = enc(p[j, zs * 2 + 1 - h])
+
+                @pl.loop(0, SLAB, step=STRIP)
+                def _(r):
+                    rows = pl.ds(pl.multiple_of(r, STRIP), STRIP)
+                    ysend[q, n, rows, :] = enc(p[j, zs * 2 + 1 - h, rows, :])
+
                 y_copy(q, n).start()
 
     def z_copy(u, i, hop):
         return remote(zsend.at[u, i], zrecv.at[u, i], z_ss.at[u, i], z_rs.at[u, i], dev(dz=hop))
 
-    def gathered(u, n, off):
+    def gathered(u, n, off, put):
         j, yfirst, other, sgn, plan = CHAINS[u]
-        v = p[j, slab(off * sgn, other)]
+        terms = []
         if yfirst:
             y_copy(YFIRST.index(j), n).wait_recv()
-            v = v + dec(yrecv[YFIRST.index(j), n])
+            terms.append(yrecv.at[YFIRST.index(j), n])
         for k, (o, hop) in enumerate(plan):
             if o - hop == off:
                 z_copy(u, k, hop * sgn).wait_recv()
-                v = v + dec(zrecv[u, k])
-        return v
+                terms.append(zrecv.at[u, k])
+        own = p.at[j, slab(off * sgn, other)]
+
+        @pl.loop(0, SLAB, step=STRIP)
+        def _(r):
+            rows = pl.ds(pl.multiple_of(r, STRIP), STRIP)
+            v = own[rows, :]
+            for term in terms:
+                v = v + dec(term[rows, :])
+            put(rows, v)
 
     def pass_on(u, i):
         sgn, plan = CHAINS[u][3:]
         off, hop = plan[i]
-        zsend[u, i] = enc(gathered(u, i, off))
+
+        def put(rows, v):
+            zsend[u, i, rows, :] = enc(v)
+
+        gathered(u, i, off, put)
         go(z_copy(u, i, hop * sgn))
 
     def f_copy(u, cc, slot):
         j, _, other, _, _ = CHAINS[u]
         dx, ll = owner(j)
         to = dev(dx, hh=1 - h if other else h, ll=ll, cc=cc)
-        return remote(fbuf.at[u, cc], frecv.at[slot, t], f_ss.at[u, cc], f_rs.at[slot, t], to)
+        return remote(fbuf.at[u, pl.ds(cc * HALF, HALF)], frecv.at[slot, t], f_ss.at[u, cc], f_rs.at[slot, t], to)
 
     def finish(u, _):
         j, yfirst, other, sgn, plan = CHAINS[u]
-        v = gathered(u, 7, 0)
-        fbuf[u, 0] = v[:HALF]
-        fbuf[u, 1] = v[HALF:]
+
+        def put(rows, v):
+            fbuf[u, rows, :] = v
+
+        gathered(u, 7, 0, put)
         for cc in range(2):
             cp = f_copy(u, cc, int(other))
             here_on = [core for core in range(2) if OWNERS[core][j] == (0, 0) and core == cc and not other]
@@ -240,7 +271,7 @@
 
             @pl.when(c == here_on[0])
             def _():
-                frecv[0, t] = fbuf[u, cc]
+                frecv[0, t] = fbuf[u, pl.ds(cc * HALF, HALF), :]
 
             late.append((c != here_on[0], cp))
 
@@ -254,7 +285,7 @@
         twice = any(ch[0] == j and ch[2] for ch in CHAINS)
         s = lax.rem(x - dx + NX, NX) * 2 + lax.rem(l + dl, 2)
         for slot in range(1 + twice):
-            cp = remote(fbuf.at[0, 0], frecv.at[slot, s], f_ss.at[0, 0], f_rs.at[slot, s], dev(cc=1 - c))
+            cp = remote(fbuf.at[0, pl.ds(0, HALF)], frecv.at[slot, s], f_ss.at[0, 0], f_rs.at[slot, s], dev(cc=1 - c))
             if dx or dl or slot:
                 cp.wait_recv()
             else:
@@ -292,7 +323,7 @@
             pltpu.VMEM((n_u, 7) + small, jnp.bfloat16),
             pltpu.VMEM((n_y, 8) + small, jnp.bfloat16),
             pltpu.VMEM((n_y, 8) + small, jnp.bfloat16),
-            pltpu.VMEM((n_u, 2, HALF, ROWB), jnp.float32),
+            pltpu.VMEM((n_u,) + small, jnp.float32),
             pltpu.VMEM((2, 8, HALF, ROWB), jnp.float32),
             dma((n_ch + 1,)),
             dma((NZ,)), dma((NZ,)),

time: 52.2 us -> 50 us (0.958)
  the two profiles are of different devices: /device:TPU:3 before, /device:TPU:1 now
where the time goes in v5:
time: 50 us; the launch traced here: 49.9 us
  Pallas kernels  47.9 us (96%)
  between operations  0.71 us (1%)
  local copies, waits for them, and re-layouts  0.7 us (1%)
  other arithmetic  0.56 us (1%)
    pallas_call x1, Pallas kernels, products_of(): pl.pallas_call(kernel, out_shape=jax.ShapeDtypeStruct((8, HALF, ROWB), jn...  47.9 us

profile of v5, /device:TPU:1, one launch (start us, length us, event | category | flops | bytes accessed | tf_op | source)
XLA Modules:
  0.0 49.9 jit_solution(804783471001566247)
XLA Ops:
  0.6 0.0 copy-start.2
  0.6 0.0 copy-start
  0.6 47.9 %summed_products.1 = f32[8,72,128]{2,1,0:T(8,128)S(1)} custom-call(bf16[512,2304]{1,0:T(8,128)(2,1)} %act.1), custom_call_target="tpu_custom_call" | custom-call | tf_op jit(solution)/shard_map/summed_products/pallas_call | solution.py:310
  48.6 0.0 copy-done.2
  48.6 0.0 copy-done
  48.6 0.3 abs_reduce_fusion
  48.9 0.0 copy-start.1
  49.0 0.2 divide_convert_fusion
  49.2 0.7 %copy.6 = bf16[72,8,128]{2,1,0:T(8,128)(2,1)} copy(bf16[72,8,128]{2,0,1:T(8,128)(2,1)S(1)} %divide_convert_fusion) | data formatting | bytes 294912
  49.9 0.0 copy-done.1
  (2 shorter events, 0.0 us)
Async XLA Ops:
  0.6 47.9 %copy-start.2 = (f32[72,8,1]{0,2,1:T(1,128)S(1)}, f32[72,8,1]{0,2,1:T(1,128)}, u32[]{:S(2)}) copy-start(f32[72,8,1]{0,2,1:T(1,128)} %param.5) | copy-start | bytes 6916
  0.6 48.0 %copy-start = (bf16[72,8,128]{2,1,0:T(8,128)(2,1)S(1)}, bf16[72,8,128]{2,1,0:T(8,128)(2,1)}, u32[]{:S(2)}) copy-start(bf16[72,8,128]{2,1,0:T(8,128)(2,1)} %param.4) | copy-start | bytes 442372
  48.9 0.9 %copy-start.1 = (f32[72,8]{0,1:T(8,128)}, f32[72,8]{0,1:T(8,128)S(1)}, u32[]{:S(2)}) copy-start(f32[72,8]{0,1:T(8,128)S(1)} %broadcast_add_fusion) | copy-start | bytes 6916
